TPU v7x, 32 devices: a whole 2x2x4 slice. The times are simulated.
32 devices in a mesh: lon: 4 (over x, core), lat: 8 (over z, y).
Axes of the slice: x: 2, y: 2, z: 4, core: 2. Of those that a mesh axis runs over, the one named last changes fastest.
Arguments:
- innovation: bfloat16 [64, 49152], P(None, ('lon', 'lat')), may hold values from -6 to 6
- owner_tile: int32 [49152, 1], P(('lon', 'lat')), may hold values from 0 to 3; in each aligned block of 1536 rows (0 to 1535, 1536 to 3071, ...) at most 768 rows name the same one
- cell_index: int32 [49152], P(('lon', 'lat')), may hold values from 0 to 8191
- length_scale: float32 [64], replicated, may hold values from 1.5 to 8
- eof_basis: bfloat16 [137, 64], replicated, may hold values from -0.75 to 0.75
Outputs:
- increment: bfloat16 [137, 512, 512], P(None, 'lat', 'lon')
Inputs may be any that keep to these rules, and one draw needn't show every extreme that they name: `owner_tile`: within the rows of one device (1536 rows, aligned blocks), no tile index appears more than 768 times, and some index appears exactly 768 times.
All inputs are finite; a program needn't handle non-finite values.
Results may differ from a plain program's by a relative error of at most 0.0076.
Values may be sent and summed in bfloat16 or wider, within the bound.
A program may use at most 64 MiB of HBM per device.

v0:
```python
import functools

import jax
import jax.numpy as jnp
from jax import lax
from jax.experimental import pallas as pl
from jax.experimental.pallas import tpu as pltpu
from jax.sharding import PartitionSpec as P

TX = 128
TY = 64


def extended(shard, sides, width):
    for axis, dim in sides:
        size, length = (lax.axis_size(axis), shard.shape[dim])
        up = [(i, (i + 1) % size) for i in range(size)]
        down = [(j, i) for i, j in up]
        last = lax.slice_in_dim(shard, length - width, length, axis=dim)
        initial = lax.slice_in_dim(shard, 0, width, axis=dim)
        before = lax.ppermute(last, axis, up)
        after = lax.ppermute(initial, axis, down)
        shard = jnp.concatenate([before, shard, after], axis=dim)
    return shard


def tap_norm(scale):
    dist = jnp.arange(-15, 16).astype(jnp.float32)
    gauss = jnp.exp(-(dist[None, :] * dist[None, :]) / (2.0 * scale[:, None] * scale[:, None]))
    return jnp.sqrt(jnp.sum(gauss * gauss, axis=1))


def tap_weight(dist, scale, norm):
    value = jnp.exp(-(dist * dist) / (2.0 * scale * scale)) / norm
    return jnp.where(jnp.abs(dist) <= 15.0, value, 0.0)


def band_matrix(scale, norm, inner, outer, offset):
    inner_pos = jnp.arange(inner).astype(jnp.float32)[:, None]
    outer_pos = jnp.arange(outer).astype(jnp.float32)[None, :]
    dist = inner_pos - offset - outer_pos
    return tap_weight(dist[None], scale[:, None, None], norm[:, None, None]).astype(jnp.bfloat16)


def slot_numbers(dest, keep, n_lon):
    hits = ((dest[:, None] == jnp.arange(n_lon, dtype=jnp.int32)[None, :]) & keep[:, None]).astype(
        jnp.int32
    )
    before = jnp.cumsum(hits, axis=0) - hits
    return jnp.sum(before * hits, axis=1)


def spread_block(part, where, width):
    cells = jnp.arange(TY * width, dtype=jnp.int32)
    grid_row = (cells // width).astype(jnp.bfloat16)
    grid_col = (cells % width).astype(jnp.bfloat16)
    onehot = (
        (where[0][:, None] == grid_row[None, :]) & (where[1][:, None] == grid_col[None, :])
    ).astype(jnp.bfloat16)
    return jnp.dot(part, onehot, preferred_element_type=jnp.float32)


def packed(innovation, owner_tile, cell_index, length_scale, eof_basis):
    n_lon = lax.axis_size("lon")
    lev, rec = innovation.shape
    cap = (2 * rec + n_lon - 1) // n_lon
    owner = owner_tile[:, 0]
    cell_row = cell_index // TX
    cell_col = cell_index % TX
    everyone = jnp.ones((rec,), jnp.bool_)
    target = owner * cap + slot_numbers(owner, everyone, n_lon)
    values = jnp.zeros((lev, n_lon * cap), jnp.bfloat16).at[:, target].set(innovation)
    coords = jnp.stack([cell_row, cell_col]).astype(jnp.bfloat16)
    places = jnp.full((2, n_lon * cap), -1.0, jnp.bfloat16).at[:, target].set(coords)
    values = values.reshape(lev, n_lon, cap)
    places = places.reshape(2, n_lon, cap)
    got_values, got_places = (
        lax.all_to_all(values, "lon", split_axis=1, concat_axis=1, tiled=True),
        lax.all_to_all(places, "lon", split_axis=1, concat_axis=1, tiled=True),
    )

    def spread_one(source, total):
        part = lax.dynamic_index_in_dim(got_values, source, 1, keepdims=False)
        where = lax.dynamic_index_in_dim(got_places, source, 1, keepdims=False)
        return total + spread_block(part, where, TX)

    summed = lax.fori_loop(0, n_lon, spread_one, jnp.zeros((lev, TY * TX), jnp.float32))
    spread = summed.astype(jnp.bfloat16).reshape(lev, TY, TX)
    padded = extended(spread, (("lon", 2),), 15)
    norm = tap_norm(length_scale)
    band_lon = band_matrix(length_scale, norm, TX + 30, TX, 15.0)
    lon_smooth = jnp.einsum(
        "cyk,ckx->cyx", padded, band_lon, preferred_element_type=jnp.float32
    ).astype(jnp.bfloat16)
    n_lat = lax.axis_size("lat")
    south = [(i, i + 1) for i in range(n_lat - 1)]
    north = [(j, i) for i, j in south]
    above = lax.ppermute(lon_smooth[:, TY - 16 :], "lat", south)
    below = lax.ppermute(lon_smooth[:, :16], "lat", north)
    column = jnp.concatenate([above, lon_smooth, below], axis=1)
    band_lat = band_matrix(length_scale, norm, TY + 32, TY, 16.0)
    smooth = jnp.einsum(
        "cky,ckx->cyx", band_lat, column, preferred_element_type=jnp.float32
    ).astype(jnp.bfloat16)
    return jnp.einsum("lc,cyx->lyx", eof_basis, smooth, preferred_element_type=jnp.float32).astype(
        jnp.bfloat16
    )


MESH = pl.DeviceIdType.MESH
HALO = 16
GROUPS = 4


def copies(ref_from, ref_to, send, recv, target):
    return pltpu.make_async_remote_copy(
        src_ref=ref_from,
        dst_ref=ref_to,
        send_sem=send,
        recv_sem=recv,
        device_id=target,
        device_id_type=MESH,
    )


def smooth_kernel(
    n_lat, innov_hbm, owner_hbm, cell_hbm, scale_hbm, eof_hbm, out_hbm, wide_hbm,
    out_ref, wide_ref, store,
    innov_ref, owner_ref, cell_ref, scale_ref, eof_ref, load, key_ref, vals, keys, picked, slots, sums, weights, band, lon, north, south,
    val_send, val_recv, key_send, key_recv, halo_send, halo_recv,
):
    lev, rec = innov_ref.shape
    levels = eof_ref.shape[1]
    loads = [
        pltpu.make_async_copy(there, here, load.at[i])
        for i, (there, here) in enumerate(
            (
                (owner_hbm, owner_ref),
                (cell_hbm, cell_ref),
                (innov_hbm, innov_ref),
                (scale_hbm, scale_ref),
                (eof_hbm, eof_ref),
            )
        )
    ]
    for copy in loads:
        copy.start()
    half = rec // 2
    me = lax.axis_index("lon")
    lat = lax.axis_index("lat")
    partner = me + 1 - 2 * (me % 2)
    across = (me + 2) % 4
    far = (partner + 2) % 4
    has_up = lat > 0
    has_down = lat < n_lat - 1

    barrier = pltpu.get_barrier_semaphore()
    for peer in (partner, across, far):
        pl.semaphore_signal(barrier, inc=1, device_id=(peer, lat), device_id_type=MESH)

    @pl.when(has_up)
    def _():
        pl.semaphore_signal(barrier, inc=1, device_id=(me, lat - 1), device_id_type=MESH)

    @pl.when(has_down)
    def _():
        pl.semaphore_signal(barrier, inc=1, device_id=(me, lat + 1), device_id_type=MESH)

    loads[0].wait()
    loads[1].wait()
    cell = cell_ref[...].reshape(1, rec)
    key_ref[...] = (cell >> 7) * 512 + owner_ref[...] * TX + (cell & (TX - 1))
    pl.semaphore_wait(barrier, 3 + has_up.astype(jnp.int32) + has_down.astype(jnp.int32))

    key_copies = [
        copies(key_ref, keys.at[i], key_send.at[i], key_recv.at[i], (peer, lat))
        for i, peer in enumerate((partner, across, far))
    ]
    parts = [pl.ds(0, half), pl.ds(half, half)]
    over = [
        copies(
            innov_hbm.at[:, parts[h]], vals.at[1, :, parts[h]],
            val_send.at[h], val_recv.at[h], (across, lat),
        )
        for h in range(2)
    ]
    beside = copies(innov_hbm, vals.at[0], val_send.at[2], val_recv.at[2], (partner, lat))
    onward = [
        copies(
            vals.at[1, :, parts[h]], vals.at[2, :, parts[h]],
            val_send.at[3 + h], val_recv.at[3 + h], (partner, lat),
        )
        for h in range(2)
    ]
    for copy in key_copies:
        copy.start()
    over[0].start()
    over[1].start()
    beside.start()

    row_of = lax.broadcasted_iota(jnp.int32, (256, rec), 0).astype(jnp.float32).astype(jnp.bfloat16)
    zero = jnp.zeros((), jnp.bfloat16)
    one = jnp.ones((), jnp.bfloat16)

    def sort_out(part, key, at):
        row = key >> 9
        rel = ((key & 511) - TX * me + HALO) & 511
        sub = (row & 7).astype(jnp.float32).astype(jnp.bfloat16)
        phase = row >> 3
        inside = (rel >= HALO) & (rel < HALO + TX)
        main = (phase & 1) * TX + rel - HALO
        for n, pair in ((0, 0), (1, 3), (3, 1), (4, 2)):
            hit = inside & ((phase >> 1) == pair)
            slots[at, n] = jnp.where(hit, main, -1).astype(jnp.float32)
        rim = jnp.where(rel < HALO, rel, rel - TX)
        rim_hit = (rel < HALO) | ((rel >= HALO + TX) & (rel < 2 * HALO + TX))
        slots[at, 2] = jnp.where(rim_hit, phase * 2 * HALO + rim, -1).astype(jnp.float32)
        values = part[...]
        for t in range(8):
            mine = sub == jnp.full((), t, jnp.bfloat16)
            picked[at, pl.ds(t * lev, lev), :] = jnp.where(mine, values, zero)

    def spread(blocks, tiles, first=False):
        got = None
        for at in blocks:
            onehot = jnp.concatenate(
                [
                    jnp.where(row_of == slots[at, n].astype(jnp.bfloat16), one, zero)
                    for n in range(*tiles)
                ],
                axis=0,
            )
            term = lax.dot_general(
                picked[at], onehot, (((1,), (1,)), ((), ())), preferred_element_type=jnp.float32
            )
            got = term if got is None else got + term
        for i in range(2 * (tiles[1] - tiles[0])):
            piece = got[:, i * TX : (i + 1) * TX]
            if first:
                sums[2 * tiles[0] + i] = piece
            else:
                sums[2 * tiles[0] + i] += piece

    loads[2].wait()
    sort_out(innov_ref, key_ref[...], 0)
    spread([0], (0, 3), True)

    line = lax.broadcasted_iota(jnp.int32, (lev, TX), 1)
    near = jnp.where(line < TX // 2, line, line - TX).astype(jnp.float32)
    loads[3].wait()
    diagonal = lax.broadcasted_iota(jnp.int32, (lev, lev), 0) == lax.broadcasted_iota(
        jnp.int32, (lev, lev), 1
    )
    scale = jnp.sum(
        jnp.where(diagonal, jnp.broadcast_to(scale_ref[...], (lev, lev)), 0.0), axis=1, keepdims=True
    )
    gauss = jnp.where(
        jnp.abs(near) <= 15.0, jnp.exp(-(near * near) / (2.0 * scale * scale)), 0.0
    )
    norm = jnp.sqrt(jnp.sum(gauss * gauss, axis=1, keepdims=True))
    weights[...] = gauss / norm
    down_at = lax.broadcasted_iota(jnp.int32, (TX, TX), 0)
    side_at = lax.broadcasted_iota(jnp.int32, (TX, TX), 1)
    straight = jnp.abs(down_at - side_at) < TX // 2
    west = side_at[:HALO] < TX // 2

    def band_one(c, carry):
        ring = pltpu.roll(
            jnp.broadcast_to(weights[pl.ds(c, 1), :], (TX, TX)), 0, 1, stride=1, stride_axis=0
        )
        band[c, :TX] = jnp.where(straight, ring, 0.0).astype(jnp.bfloat16)
        rim = jnp.concatenate(
            [jnp.where(west, ring[TX - HALO :], 0.0), jnp.where(west, 0.0, ring[:HALO])], axis=0
        ).astype(jnp.bfloat16)
        for t in range(4):
            band[c, TX + 2 * HALO * t : TX + 2 * HALO * (t + 1)] = rim
        return carry

    lax.fori_loop(0, lev, band_one, 0, unroll=4)

    key_copies[0].wait_recv()
    beside.wait_recv()
    sort_out(vals.at[0], keys[0], 1)
    spread([1], (0, 3))
    for h in range(2):
        over[h].wait_recv()
        onward[h].start()
    key_copies[1].wait_recv()
    sort_out(vals.at[1], keys[1], 2)
    spread([2], (0, 3))
    key_copies[2].wait_recv()
    for h in range(2):
        onward[h].wait_recv()
    sort_out(vals.at[2], keys[2], 3)
    spread([3], (0, 3))

    lane = lax.broadcasted_iota(jnp.int32, (8, TX), 1) >> 5
    width = lev // GROUPS
    spot = (0, 1, 6, 7, 8, 9, 2, 3)

    def lon_rows(c, phases):
        rows = pl.ds(c, 8, stride=lev)
        main = [sums[spot[p], rows, :] for p in phases]
        rim = [jnp.where(lane == p % 4, sums[4 + p // 4, rows, :], 0.0) for p in phases]
        left = jnp.concatenate(
            [jnp.concatenate(main, axis=0), jnp.concatenate(rim, axis=0)], axis=1
        ).astype(jnp.bfloat16)
        return jnp.dot(left, band[c], preferred_element_type=jnp.float32).astype(jnp.bfloat16)

    def lon_one(c, carry):
        got = lon_rows(c, (0, 1, 6, 7))
        lon[c, :HALO] = got[:HALO]
        lon[c, TY - HALO :] = got[HALO:]
        return carry

    def mid_one(c, carry):
        lon[c, HALO : TY - HALO] = lon_rows(c, (2, 3, 4, 5))
        return carry

    def inner_one(c, carry):
        out_ref[c, HALO : TY - HALO] = jnp.dot(
            band[c, HALO : TY - HALO, :TY], lon[c], preferred_element_type=jnp.float32
        ).astype(jnp.bfloat16)
        return carry

    ups, downs = [], []
    for g in range(GROUPS):
        lax.fori_loop(g * width, (g + 1) * width, lon_one, 0, unroll=4)
        chans = pl.ds(g * width, width)
        up = copies(
            lon.at[chans, pl.ds(0, HALO), :], south.at[chans],
            halo_send.at[0, g], halo_recv.at[0, g], (me, lat - 1),
        )
        down = copies(
            lon.at[chans, pl.ds(TY - HALO, HALO), :], north.at[chans],
            halo_send.at[1, g], halo_recv.at[1, g], (me, lat + 1),
        )
        ups.append(up)
        downs.append(down)

        @pl.when(has_up)
        def _(up=up):
            up.start()

        @pl.when(has_down)
        def _(down=down):
            down.start()

    @pl.when(jnp.logical_not(has_up))
    def _():
        north[...] = jnp.zeros_like(north)

    @pl.when(jnp.logical_not(has_down))
    def _():
        south[...] = jnp.zeros_like(south)

    spread([0, 1, 2, 3], (3, 5), True)
    lax.fori_loop(0, lev, mid_one, 0, unroll=4)
    lax.fori_loop(0, lev, inner_one, 0, unroll=4)

    loads[4].wait()
    copy_of = lax.broadcasted_iota(jnp.int32, (lev, 8 * lev), 1) >> 3
    chan = lax.broadcasted_iota(jnp.int32, (lev, 8 * lev), 0)
    repeat = jnp.where(copy_of == chan, 1.0, 0.0).astype(jnp.bfloat16)
    flat = lax.dot_general(
        eof_ref[...], repeat, (((0,), (0,)), ((), ())), preferred_element_type=jnp.float32
    ).astype(jnp.bfloat16)
    row = lax.broadcasted_iota(jnp.int32, (8 * levels, levels), 0) >> 3
    level = lax.broadcasted_iota(jnp.int32, (8 * levels, levels), 1)
    down_all = jnp.where(row == level, 1.0, 0.0).astype(jnp.bfloat16)
    tall = jnp.dot(down_all, flat, preferred_element_type=jnp.float32)
    y_out = lax.broadcasted_iota(jnp.int32, (8 * levels, 8 * lev), 0) & 7
    y_in = lax.broadcasted_iota(jnp.int32, (8 * levels, 8 * lev), 1) & 7
    wide_ref[...] = jnp.where(y_out == y_in, tall, 0.0).astype(jnp.bfloat16)
    stores = [pltpu.make_async_copy(wide_ref, wide_hbm, store.at[GROUPS])]
    stores[0].start()

    def lat_one(c, carry):
        own = lon[c]
        column = jnp.concatenate(
            [
                jnp.concatenate([north[c], own[: 2 * HALO]], axis=0),
                jnp.concatenate([own[TY - 2 * HALO :], south[c]], axis=0),
            ],
            axis=1,
        )
        got = jnp.dot(
            band[c, HALO : 2 * HALO, : 3 * HALO], column, preferred_element_type=jnp.float32
        ).astype(jnp.bfloat16)
        out_ref[c, :HALO] = got[:, :TX]
        out_ref[c, TY - HALO :] = got[:, TX:]
        return carry

    for g in range(GROUPS):

        @pl.when(has_up)
        def _(g=g):
            downs[g].wait_recv()

        @pl.when(has_down)
        def _(g=g):
            ups[g].wait_recv()

        lax.fori_loop(g * width, (g + 1) * width, lat_one, 0, unroll=4)
        chans = pl.ds(g * width, width)
        stores.append(pltpu.make_async_copy(out_ref.at[chans], out_hbm.at[chans], store.at[g]))
        stores[-1].start()

    for copy in stores:
        copy.wait()
    for copy in key_copies + over + [beside] + onward:
        copy.wait_send()
    for g in range(GROUPS):

        @pl.when(has_up)
        def _(g=g):
            ups[g].wait_send()

        @pl.when(has_down)
        def _(g=g):
            downs[g].wait_send()


def mix_kernel(wide_ref, field_ref, out_ref):
    levels = out_ref.shape[0]
    lev = field_ref.shape[0]
    field = field_ref[...].astype(jnp.float32)
    right = jnp.concatenate(
        [field[:, y : y + 8].reshape(8 * lev, TX) for y in range(0, 32, 8)], axis=1
    ).astype(jnp.bfloat16)
    got = jnp.dot(wide_ref[...], right, preferred_element_type=jnp.float32)
    out_ref[...] = jnp.concatenate(
        [got[:, x : x + TX].reshape(levels, 8, TX) for x in range(0, 4 * TX, TX)], axis=1
    ).astype(jnp.bfloat16)


def gathered(innovation, owner_tile, cell_index, length_scale, eof_basis):
    n_lat = lax.axis_size("lat")
    lev, rec = innovation.shape
    levels = eof_basis.shape[0]
    hbm = pl.BlockSpec(memory_space=pltpu.HBM)
    smooth, wide = pl.pallas_call(
        functools.partial(smooth_kernel, n_lat),
        out_shape=(
            jax.ShapeDtypeStruct((lev, TY, TX), jnp.bfloat16),
            jax.ShapeDtypeStruct((8 * levels, 8 * lev), jnp.bfloat16),
        ),
        in_specs=[hbm] * 5,
        out_specs=(hbm, hbm),
        scratch_shapes=[
            pltpu.VMEM((lev, TY, TX), jnp.bfloat16),
            pltpu.VMEM((8 * levels, 8 * lev), jnp.bfloat16),
            pltpu.SemaphoreType.DMA((GROUPS + 1,)),
            pltpu.VMEM((lev, rec), jnp.bfloat16),
            pltpu.VMEM((1, rec), jnp.int32),
            pltpu.VMEM((rec,), jnp.int32),
            pltpu.VMEM((1, lev), jnp.float32),
            pltpu.VMEM((lev, levels), jnp.bfloat16),
            pltpu.SemaphoreType.DMA((5,)),
            pltpu.VMEM((1, rec), jnp.int32),
            pltpu.VMEM((3, lev, rec), jnp.bfloat16),
            pltpu.VMEM((3, 1, rec), jnp.int32),
            pltpu.VMEM((4, 8 * lev, rec), jnp.bfloat16),
            pltpu.VMEM((4, 5, 1, rec), jnp.float32),
            pltpu.VMEM((10, 8 * lev, TX), jnp.float32),
            pltpu.VMEM((lev, TX), jnp.float32),
            pltpu.VMEM((lev, 2 * TX, TX), jnp.bfloat16),
            pltpu.VMEM((lev, TY, TX), jnp.bfloat16),
            pltpu.VMEM((lev, HALO, TX), jnp.bfloat16),
            pltpu.VMEM((lev, HALO, TX), jnp.bfloat16),
            pltpu.SemaphoreType.DMA((5,)),
            pltpu.SemaphoreType.DMA((5,)),
            pltpu.SemaphoreType.DMA((3,)),
            pltpu.SemaphoreType.DMA((3,)),
            pltpu.SemaphoreType.DMA((2, GROUPS)),
            pltpu.SemaphoreType.DMA((2, GROUPS)),
        ],
        compiler_params=pltpu.CompilerParams(
            collective_id=0, has_side_effects=True, vmem_limit_bytes=58 * 1024 * 1024
        ),
        cost_estimate=pl.CostEstimate(
            flops=2 * 8 * lev * 4 * rec * 1280, bytes_accessed=8 * 1024 * 1024, transcendentals=0
        ),
    )(innovation, owner_tile.reshape(1, rec), cell_index, length_scale.reshape(1, lev), eof_basis.T)
    return pl.pallas_call(
        mix_kernel,
        out_shape=jax.ShapeDtypeStruct((levels, TY, TX), jnp.bfloat16),
        grid=(TY // 32,),
        in_specs=[
            pl.BlockSpec((8 * levels, 8 * lev), lambda g: (0, 0)),
            pl.BlockSpec((lev, 32, TX), lambda g: (0, g, 0)),
        ],
        out_specs=pl.BlockSpec((levels, 32, TX), lambda g: (0, g, 0)),
        compiler_params=pltpu.CompilerParams(vmem_limit_bytes=58 * 1024 * 1024),
    )(wide, smooth)


def solution(mesh):
    in_specs = (P(None, ("lon", "lat")), P(("lon", "lat"), None), P(("lon", "lat")), P(), P())
    out_specs = P(None, "lat", "lon")
    local = gathered if mesh.shape["lon"] == 4 else packed
    return jax.shard_map(local, mesh=mesh, in_specs=in_specs, out_specs=out_specs, check_vma=False)
```

profile of v0, /device:TPU:0, one launch (start us, length us, event | category | flops | bytes accessed | tf_op | source)
XLA Modules:
  0.0 32.5 jit_solution(5996056884873299007)
XLA Ops:
  0.0 28.5 %shard_map.55 = (bf16[64,64,128]{2,1,0:T(8,128)(2,1)}, bf16[1096,512]{1,0:T(8,128)(2,1)}) custom-call(bf16[64,1536]{1,0:T(8,128)(2,1)} %innov_hbm.1, s32[1,1536]{1,0:T(1,128)} %bitcast.4, s32[1536]{0:T(1024)} %cell_hbm.1, f32[1,64]{1,0:T(1,128)} %bitcast.5, bf16[64,137]{1,0:T(8,128)(2,1)} %bitcast.3), custom_call_target="tpu_custom_call" | custom-call | flops 8053063680 | bytes 8388608 | tf_op jit(solution)/shard_map/pallas_call | solution.py:442
  28.6 4.0 %shard_map.56 = bf16[137,64,128]{2,1,0:T(8,128)(2,1)} custom-call(bf16[1096,512]{1,0:T(8,128)(2,1)} %get-tuple-element.7.wide_ref, bf16[64,64,128]{2,1,0:T(8,128)(2,1)} %get-tuple-element.8.field_ref), custom_call_target="tpu_custom_call" | custom-call | tf_op jit(solution)/shard_map/pallas_call | solution.py:485
where the time goes:
time: 32.7 us; the launch traced here: 32.5 us
  Pallas kernels  32.5 us (99%)
    pallas_call x1, Pallas kernels, gathered(): pl.pallas_call(functools.partial(smooth_kernel, n_lat), out_shape=(jax.Sh...  28.5 us
    pallas_call x1, Pallas kernels, gathered(): pl.pallas_call(mix_kernel, out_shape=jax.ShapeDtypeStruct((levels, TY, TX...  3.95 us

commit v1 on v0

--- a/solution.py
+++ b/solution.py
@@ -126,7 +126,7 @@
 def smooth_kernel(
     n_lat, innov_hbm, owner_hbm, cell_hbm, scale_hbm, eof_hbm, out_hbm, wide_hbm,
     out_ref, wide_ref, store,
-    innov_ref, owner_ref, cell_ref, scale_ref, eof_ref, load, key_ref, vals, keys, picked, slots, sums, weights, band, lon, north, south,
+    innov_ref, owner_ref, cell_ref, scale_ref, eof_ref, load, key_ref, vals, keys, picked, codes, sums, weights, band, lon, north, south,
     val_send, val_recv, key_send, key_recv, halo_send, halo_recv,
 ):
     lev, rec = innov_ref.shape
@@ -198,9 +198,8 @@
     over[1].start()
     beside.start()
 
-    row_of = lax.broadcasted_iota(jnp.int32, (256, rec), 0).astype(jnp.float32).astype(jnp.bfloat16)
+    column = lax.broadcasted_iota(jnp.int32, (rec, TX), 1).astype(jnp.float32)
     zero = jnp.zeros((), jnp.bfloat16)
-    one = jnp.ones((), jnp.bfloat16)
 
     def sort_out(part, key, at):
         row = key >> 9
@@ -208,13 +207,13 @@
         sub = (row & 7).astype(jnp.float32).astype(jnp.bfloat16)
         phase = row >> 3
         inside = (rel >= HALO) & (rel < HALO + TX)
-        main = (phase & 1) * TX + rel - HALO
-        for n, pair in ((0, 0), (1, 3), (3, 1), (4, 2)):
-            hit = inside & ((phase >> 1) == pair)
-            slots[at, n] = jnp.where(hit, main, -1).astype(jnp.float32)
-        rim = jnp.where(rel < HALO, rel, rel - TX)
+        pair = phase >> 1
+        start = jnp.where(pair == 0, 0, jnp.where(pair == 3, 2 * TX, 4 * TX + pair * 2 * TX))
+        main = start + (phase & 1) * TX + rel - HALO
         rim_hit = (rel < HALO) | ((rel >= HALO + TX) & (rel < 2 * HALO + TX))
-        slots[at, 2] = jnp.where(rim_hit, phase * 2 * HALO + rim, -1).astype(jnp.float32)
+        rim = 4 * TX + phase * 2 * HALO + jnp.where(rel < HALO, rel, rel - TX)
+        code = jnp.where(inside, main, jnp.where(rim_hit, rim, -1)).astype(jnp.float32)
+        codes[at] = jnp.broadcast_to(code, (TX, rec)).T
         values = part[...]
         for t in range(8):
             mine = sub == jnp.full((), t, jnp.bfloat16)
@@ -223,16 +222,15 @@
     def spread(blocks, tiles, first=False):
         got = None
         for at in blocks:
+            code = codes[at]
             onehot = jnp.concatenate(
                 [
-                    jnp.where(row_of == slots[at, n].astype(jnp.bfloat16), one, zero)
-                    for n in range(*tiles)
+                    jnp.where(code == column + float(i * TX), 1.0, 0.0).astype(jnp.bfloat16)
+                    for i in range(2 * tiles[0], 2 * tiles[1])
                 ],
-                axis=0,
+                axis=1,
             )
-            term = lax.dot_general(
-                picked[at], onehot, (((1,), (1,)), ((), ())), preferred_element_type=jnp.float32
-            )
+            term = jnp.dot(picked[at], onehot, preferred_element_type=jnp.float32)
             got = term if got is None else got + term
         for i in range(2 * (tiles[1] - tiles[0])):
             piece = got[:, i * TX : (i + 1) * TX]
@@ -325,7 +323,7 @@
 
     ups, downs = [], []
     for g in range(GROUPS):
-        lax.fori_loop(g * width, (g + 1) * width, lon_one, 0, unroll=4)
+        lax.fori_loop(g * width, (g + 1) * width, lon_one, 0, unroll=8)
         chans = pl.ds(g * width, width)
         up = copies(
             lon.at[chans, pl.ds(0, HALO), :], south.at[chans],
@@ -355,8 +353,8 @@
         south[...] = jnp.zeros_like(south)
 
     spread([0, 1, 2, 3], (3, 5), True)
-    lax.fori_loop(0, lev, mid_one, 0, unroll=4)
-    lax.fori_loop(0, lev, inner_one, 0, unroll=4)
+    lax.fori_loop(0, lev, mid_one, 0, unroll=8)
+    lax.fori_loop(0, lev, inner_one, 0, unroll=8)
 
     loads[4].wait()
     copy_of = lax.broadcasted_iota(jnp.int32, (lev, 8 * lev), 1) >> 3
@@ -401,7 +399,7 @@
         def _(g=g):
             ups[g].wait_recv()
 
-        lax.fori_loop(g * width, (g + 1) * width, lat_one, 0, unroll=4)
+        lax.fori_loop(g * width, (g + 1) * width, lat_one, 0, unroll=8)
         chans = pl.ds(g * width, width)
         stores.append(pltpu.make_async_copy(out_ref.at[chans], out_hbm.at[chans], store.at[g]))
         stores[-1].start()
@@ -461,7 +459,7 @@
             pltpu.VMEM((3, lev, rec), jnp.bfloat16),
             pltpu.VMEM((3, 1, rec), jnp.int32),
             pltpu.VMEM((4, 8 * lev, rec), jnp.bfloat16),
-            pltpu.VMEM((4, 5, 1, rec), jnp.float32),
+            pltpu.VMEM((4, rec, TX), jnp.float32),
             pltpu.VMEM((10, 8 * lev, TX), jnp.float32),
             pltpu.VMEM((lev, TX), jnp.float32),
             pltpu.VMEM((lev, 2 * TX, TX), jnp.bfloat16),

time: 32.7 us -> 31.7 us (0.969)
  the two profiles are of different devices: /device:TPU:0 before, /device:TPU:25 now
where the time goes in v1:
time: 31.7 us; the launch traced here: 31.5 us
  Pallas kernels  31.5 us (99%)
    pallas_call x1, Pallas kernels, gathered(): pl.pallas_call(functools.partial(smooth_kernel, n_lat), out_shape=(jax.Sh...  27.6 us
    pallas_call x1, Pallas kernels, gathered(): pl.pallas_call(mix_kernel, out_shape=jax.ShapeDtypeStruct((levels, TY, TX...  3.95 us

profile of v1, /device:TPU:25, one launch (start us, length us, event | category | flops | bytes accessed | tf_op | source)
XLA Modules:
  0.0 31.5 jit_solution(1695608354220849398)
XLA Ops:
  0.0 27.6 %shard_map.55 = (bf16[64,64,128]{2,1,0:T(8,128)(2,1)}, bf16[1096,512]{1,0:T(8,128)(2,1)}) custom-call(bf16[64,1536]{1,0:T(8,128)(2,1)} %innov_hbm.1, s32[1,1536]{1,0:T(1,128)} %bitcast.4, s32[1536]{0:T(1024)} %cell_hbm.1, f32[1,64]{1,0:T(1,128)} %bitcast.5, bf16[64,137]{1,0:T(8,128)(2,1)} %bitcast.3), custom_call_target="tpu_custom_call" | custom-call | flops 8053063680 | bytes 8388608 | tf_op jit(solution)/shard_map/pallas_call | solution.py:440
  27.6 3.9 %shard_map.56 = bf16[137,64,128]{2,1,0:T(8,128)(2,1)} custom-call(bf16[1096,512]{1,0:T(8,128)(2,1)} %get-tuple-element.7.wide_ref, bf16[64,64,128]{2,1,0:T(8,128)(2,1)} %get-tuple-element.8.field_ref), custom_call_target="tpu_custom_call" | custom-call | tf_op jit(solution)/shard_map/pallas_call | solution.py:483

commit v2 on v1

--- a/solution.py
+++ b/solution.py
@@ -109,7 +109,7 @@
 
 MESH = pl.DeviceIdType.MESH
 HALO = 16
-GROUPS = 4
+GROUPS = 8
 
 
 def copies(ref_from, ref_to, send, recv, target):

time: 31.7 us -> 34.2 us (1.079)
  the two profiles are of different devices: /device:TPU:25 before, /device:TPU:0 now
where the time goes in v2:
time: 34.2 us; the launch traced here: 34 us
  Pallas kernels  34 us (99%)
    pallas_call x1, Pallas kernels, gathered(): pl.pallas_call(functools.partial(smooth_kernel, n_lat), out_shape=(jax.Sh...  30 us
    pallas_call x1, Pallas kernels, gathered(): pl.pallas_call(mix_kernel, out_shape=jax.ShapeDtypeStruct((levels, TY, TX...  3.95 us

profile of v2, /device:TPU:0, one launch (start us, length us, event | category | flops | bytes accessed | tf_op | source)
XLA Modules:
  0.0 34.0 jit_solution(12860459472111517621)
XLA Ops:
  0.0 30.0 %shard_map.55 = (bf16[64,64,128]{2,1,0:T(8,128)(2,1)}, bf16[1096,512]{1,0:T(8,128)(2,1)}) custom-call(bf16[64,1536]{1,0:T(8,128)(2,1)} %innov_hbm.1, s32[1,1536]{1,0:T(1,128)} %bitcast.4, s32[1536]{0:T(1024)} %cell_hbm.1, f32[1,64]{1,0:T(1,128)} %bitcast.5, bf16[64,137]{1,0:T(8,128)(2,1)} %bitcast.3), custom_call_target="tpu_custom_call" | custom-call | flops 8053063680 | bytes 8388608 | tf_op jit(solution)/shard_map/pallas_call | solution.py:440
  30.0 3.9 %shard_map.56 = bf16[137,64,128]{2,1,0:T(8,128)(2,1)} custom-call(bf16[1096,512]{1,0:T(8,128)(2,1)} %get-tuple-element.7.wide_ref, bf16[64,64,128]{2,1,0:T(8,128)(2,1)} %get-tuple-element.8.field_ref), custom_call_target="tpu_custom_call" | custom-call | tf_op jit(solution)/shard_map/pallas_call | solution.py:483
